TPU v7x, 32 devices: a whole 2x2x4 slice. The times are simulated.
32 devices in a mesh: front: 2 (over y), row: 2 (over x), col: 8 (over z, core).
Axes of the slice: x: 2, y: 2, z: 4, core: 2. Of those that a mesh axis runs over, the one named last changes fastest.
Arguments:
- front_orig: bfloat16 [2, 12288, 12288], P('front', 'row', 'col'), as said below
- child_update: bfloat16 [8192, 32768], P(('front', 'row'), 'col'), as said below
- tile_map: int32 [2, 2, 64], replicated, may hold values from 0 to 95, as said below
Outputs:
- update: float32 [2, 12288, 12288], P('front', 'row', 'col')
- factor: float32 [2, 12288, 512], P('front', 'row')
Inputs may be any that keep to these rules, and one draw needn't show every extreme that they name: For every f and c, tile_map[f, c] is one-to-one. tile_map[f, c, i] mod 8 depends only on i mod 8 and takes each of its 8 values once over 8 consecutive i; tile_map[f, c, i] mod 2 depends only on i mod 2. `front_orig`: each front is symmetric in logical order. `child_update`: each child's 8192 x 8192 matrix is symmetric.
All inputs are finite; a program needn't handle non-finite values.
Results may differ from a plain program's by a relative error of at most 0.0009.
Values may be sent and summed in bfloat16 or wider, within the bound.
A program may use at most 192 MiB of HBM per device.

v0:
```python
import jax
import jax.numpy as jnp
from jax import lax
from jax.sharding import PartitionSpec as P

TILE = 128
PANELS = 2
PANEL = 256
NT = 96
NCT = 64


def from_partner(block, axis, apart):
    count = lax.axis_size(axis)
    route = []
    for low in range(count):
        high = low | 1 << apart
        if high != low and high < count:
            route += [(low, high), (high, low)]
    return lax.ppermute(block, axis, route)


def broadcast(block, axis, holder):
    block = jnp.where(lax.axis_index(axis) == holder, block, jnp.zeros_like(block))
    return lax.psum(block, axis)


def dot_high(left_mat, right_mat):
    return lax.dot_general(
        left_mat,
        right_mat,
        (((1,), (1,)), ((), ())),
        precision=lax.Precision.HIGHEST,
        preferred_element_type=jnp.float32,
    )


def per_device(front_orig, child_update, tile_map):
    row_count = lax.axis_size("row")
    col_count = lax.axis_size("col")
    front_id = lax.axis_index("front")
    row_id = lax.axis_index("row")
    col_id = lax.axis_index("col")
    local_rt = NT // row_count
    local_ct = NT // col_count
    band_rows = NCT // (2 * row_count)
    band_cols = 4 * NCT // col_count
    cap_rows = max(1, band_rows // row_count)
    cap_cols = max(1, band_cols // col_count)
    capacity = cap_rows * cap_cols
    half_cols = col_count // 2
    quarter = col_count // 4
    peer_count = row_count * col_count
    tile_stack = (
        child_update.reshape(band_rows, TILE, band_cols, TILE)
        .transpose(0, 2, 1, 3)
        .reshape(band_rows * band_cols, TILE, TILE)
    )
    along_rows = jnp.arange(band_rows)[:, None]
    along_cols = jnp.arange(band_cols)[None, :]
    child_no = col_id // quarter
    sender_map = tile_map[child_no // 2, child_no % 2]
    mapped_rows = sender_map[(front_id * row_count + row_id) * band_rows + along_rows]
    mapped_cols = sender_map[col_id % quarter * band_cols + along_cols]
    destination = mapped_rows % row_count * col_count + mapped_cols % col_count
    slot_no = along_rows // row_count * cap_cols + along_cols // col_count
    placement = (destination * capacity + slot_no).reshape(-1)
    outgoing = (
        jnp.zeros((peer_count * capacity, TILE, TILE), jnp.bfloat16).at[placement].set(tile_stack)
    )
    arrived = lax.all_to_all(outgoing, ("row", "col"), split_axis=0, concat_axis=0, tiled=True)
    arrived = arrived.reshape(row_count, 2, half_cols, capacity, TILE, TILE)
    kept = lax.dynamic_index_in_dim(arrived, front_id, 1, keepdims=False)
    leaving = lax.dynamic_index_in_dim(arrived, 1 - front_id, 1, keepdims=False)
    incoming = from_partner(leaving, "front", 0)
    slot_count = 2 * row_count * half_cols * capacity
    received = jnp.stack([kept, incoming]).reshape(slot_count, TILE, TILE)
    own_maps = lax.dynamic_index_in_dim(tile_map, front_id, 0, keepdims=False)
    source_side = jnp.arange(2)[:, None, None, None, None]
    source_row = jnp.arange(row_count)[None, :, None, None, None]
    source_col = jnp.arange(half_cols)[None, None, :, None, None]
    tile_row = jnp.arange(band_rows)[None, None, None, :, None]
    tile_col = jnp.arange(band_cols)[None, None, None, None, :]
    source_front = jnp.where(source_side == 0, front_id, 1 - front_id)
    sibling = source_col // quarter
    got_rows = own_maps[sibling, (source_front * row_count + source_row) * band_rows + tile_row]
    got_cols = own_maps[sibling, source_col % quarter * band_cols + tile_col]
    is_mine = (got_rows % row_count == row_id) & (got_cols % col_count == col_id)
    position = (
        ((source_side * row_count + source_row) * half_cols + source_col) * capacity
        + tile_row // row_count * cap_cols
        + tile_col // col_count
    )
    target = got_rows // row_count * local_ct + got_cols // col_count
    spare_tile = local_rt * local_ct
    position = jnp.where(is_mine, position, slot_count)
    slot_table = (
        jnp.full((slot_count,), spare_tile, jnp.int32)
        .at[position.reshape(-1)]
        .set(target.reshape(-1), mode="drop")
    )
    tile_sums = (
        front_orig[0]
        .astype(jnp.float32)
        .reshape(local_rt, TILE, local_ct, TILE)
        .transpose(0, 2, 1, 3)
        .reshape(spare_tile, TILE, TILE)
    )
    tile_sums = jnp.concatenate([tile_sums, jnp.zeros((1, TILE, TILE), jnp.float32)])
    tile_sums = tile_sums.at[slot_table].add(received.astype(jnp.float32))
    front_mat = (
        tile_sums[:spare_tile]
        .reshape(local_rt, local_ct, TILE, TILE)
        .transpose(0, 2, 1, 3)
        .reshape(local_rt * TILE, local_ct * TILE)
    )
    row_tiles = jnp.repeat(row_id + row_count * jnp.arange(local_rt), TILE)
    ratio = col_count // row_count
    offset = (col_id - row_id) // row_count % ratio
    identity = jnp.eye(PANEL, dtype=jnp.float32)
    columns = []
    for panel_no in range(PANELS):
        halves = []
        for side_no in range(2):
            halves.append(broadcast(front_mat[:, :TILE], "col", 2 * panel_no + side_no))
        strip_cols = jnp.concatenate(halves, axis=1)
        block_rows = []
        for side_no in range(2):
            tile_no = 2 * panel_no + side_no
            local_no = tile_no // row_count
            rows_here = strip_cols[local_no * TILE : (local_no + 1) * TILE]
            block_rows.append(jnp.where(row_id == tile_no % row_count, rows_here, 0.0))
        diagonal = lax.psum(jnp.concatenate(block_rows, axis=0), "row")
        lower_f = jnp.linalg.cholesky(diagonal)
        inverse = jax.scipy.linalg.solve_triangular(lower_f, identity, lower=True)
        panel_cols = dot_high(strip_cols, inverse)
        panel_cols = jnp.where((row_tiles >= 2 * panel_no)[:, None], panel_cols, 0.0)
        columns.append(panel_cols)
        trail_rows = jnp.where((row_tiles >= 2 * panel_no + 2)[:, None], panel_cols, 0.0)
        picked = lax.dynamic_index_in_dim(
            trail_rows.reshape(local_ct, ratio, TILE, PANEL), offset, 1, keepdims=False
        )
        picked = picked.reshape(local_ct * TILE, PANEL)
        trail_cols = broadcast(picked.astype(jnp.bfloat16), "row", col_id % row_count).astype(
            picked.dtype
        )
        front_mat = front_mat - dot_high(trail_rows, trail_cols)
    return (front_mat[None], jnp.concatenate(columns, axis=1)[None])


def solution(mesh):
    placed = (P("front", "row", "col"), P(("front", "row"), "col"), P())
    return jax.shard_map(
        per_device,
        mesh=mesh,
        in_specs=placed,
        out_specs=(P("front", "row", "col"), P("front", "row", None)),
        check_vma=False,
    )
```

profile of v0, /device:TPU:25, one launch (start us, length us, event | category | flops | bytes accessed | tf_op | source)
XLA Modules:
  0.0 1581.7 jit_solution(6701060575740899786)
XLA Ops:
  37.5 73.0 %scatter_fusion = bf16[512,128,128]{2,1,0:T(8,128)(2,1)} fusion(bf16[512,128,128]{2,1,0:T(8,128)(2,1)} %broadcast_in_dim.113, s32[512]{0:T(512)S(1)} %bitcast.157, bf16[512,128,128]{2,1,0:T(8,128)(2,1)} %bitcast.148), kind=kCustom, calls=%fused_computation.5 | custom fusion | bytes 50333696 | tf_op jit(solution)/shard_map/scatter | solution.py:69
  116.9 339.7 %all-to-all-done = bf16[512,128,128]{2,1,0:T(8,128)(2,1)} async-done(((bf16[512,128,128]{2,1,0:T(8,128)(2,1)}), bf16[512,128,128]{2,1,0:T(8,128)(2,1)}, u32[]{:S(2)}, u32[]{:S(2)}) %all-to-all-start) | async-done | bytes 16777248 | tf_op jit(solution)/shard_map/all_to_all | solution.py:71
  475.3 24.6 %copy.18 = bf16[1,6144,1536]{1,2,0:T(8,128)(2,1)} copy(bf16[1,6144,1536]{2,1,0:T(8,128)(2,1)} %param.6) | data formatting | bytes 37748736 | tf_op args[0]
  499.9 18.3 %copy.29 = bf16[192,8,48,128]{3,2,1,0:T(8,128)(2,1)} copy(bf16[192,8,48,128]{3,1,2,0:T(8,128)(2,1)} %bitcast.146) | data formatting | bytes 37748736
  518.2 26.0 %copy.19 = bf16[48,12,128,128]{3,2,1,0:T(8,128)(2,1)} copy(bf16[48,12,128,128]{2,0,3,1:T(8,128)(2,1)} %bitcast.145) | data formatting | bytes 37748736 | tf_op jit(solution)/shard_map/transpose | solution.py:106
  544.2 30.6 %scatter_custom_fusion = s32[512]{0:T(512)S(1)} fusion(s32[8192]{0:T(1024)S(1)} %bitcast.156, s32[8192]{0:T(1024)S(1)} %reshape.858, s32[]{:T(128)} %constant.299.clone.1), kind=kCustom, calls=%fused_computation.170 | custom fusion | bytes 2052 | tf_op jit(solution)/shard_map/scatter | solution.py:100
  574.8 20.9 %pad_convert_fusion = f32[577,128,128]{2,1,0:T(8,128)} fusion(bf16[576,128,128]{2,1,0:T(8,128)(2,1)} %bitcast.147), kind=kLoop, calls=%fused_computation.14 | loop fusion | flops 9453568 | bytes 56688640 | tf_op jit(solution)/shard_map/concatenate | solution.py:109
  595.8 54.8 %collective-permute-done = bf16[2,4,32,128,128]{4,3,2,1,0:T(8,128)(2,1)} collective-permute-done((bf16[2,4,32,128,128]{4,3,2,1,0:T(8,128)(2,1)}, bf16[2,4,32,128,128]{4,3,2,1,0:T(8,128)(2,1)}, u32[]{:S(2)}, u32[]{:S(2)}) %collective-permute-start) | collective-permute-done | bytes 8388640 | tf_op jit(solution)/shard_map/ppermute | solution.py:20
  670.7 103.9 %scatter_fusion.1 = f32[577,128,128]{2,1,0:T(8,128)} fusion(f32[577,128,128]{2,1,0:T(8,128)} %pad_convert_fusion, s32[512]{0:T(512)S(1)} %compare_select_fusion.3, f32[512,128,128]{2,1,0:T(8,128)} %bitcast_convert_fusion), kind=kCustom, calls=%fused_computation.6 | custom fusion | flops 8388608 | bytes 100665344 | tf_op jit(solution)/shard_map/scatter-add | solution.py:110
  774.6 27.4 %slice.82 = f32[576,128,128]{2,1,0:T(8,128)} slice(f32[577,128,128]{2,1,0:T(8,128)} %scatter_fusion.1), slice={[0:576], [0:128], [0:128]} | slice | bytes 75497472 | tf_op jit(solution)/shard_map/slice | solution.py:112
  802.1 36.9 %copy.21 = f32[48,128,12,128]{1,0,3,2:T(8,128)} copy(f32[48,128,12,128]{3,1,2,0:T(8,128)} %bitcast.144) | data formatting | bytes 75497472 | tf_op jit(solution)/shard_map/transpose | solution.py:114
  839.0 22.2 %copy.35 = f32[192,8,48,128]{3,1,2,0:T(8,128)S(1)} copy(f32[192,8,48,128]{3,2,1,0:T(8,128)} %bitcast.142) | data formatting | bytes 75497472
  864.9 158.1 %all-reduce.21.cloned.1.call-done = (f32[6144,128]{0,1:T(8,128)}, f32[6144,128]{0,1:T(8,128)}) async-done(((f32[6144,128]{0,1:T(8,128)}, f32[6144,128]{0,1:T(8,128)}), (f32[6144,128]{0,1:T(8,128)}, f32[6144,128]{0,1:T(8,128)})) %all-reduce.21.cloned.1.call-update) | async-done | bytes 6291472 | tf_op jit(solution)/shard_map/psum | solution.py:25
  1030.0 23.3 %all-reduce.11.cloned.1.call-done = f32[256,256]{0,1:T(8,128)} async-done(((f32[256,256]{0,1:T(8,128)}), f32[256,256]{0,1:T(8,128)}) %all-reduce.11.cloned.1.call-update) | async-done | bytes 262160 | tf_op jit(solution)/shard_map/psum | solution.py:133
  1096.3 19.7 %custom-call.18 = f32[2,128,128]{1,2,0:T(8,128)S(1)} custom-call(f32[2,128,128]{2,1,0:T(8,128)S(1)} %get-tuple-element.18), custom_call_target="InvertDiagBlocksLowerTriangular" | custom-call | tf_op jit(solution)/shard_map/jit(_solve_triangular)/triangular_solve | solution.py:135
  1116.9 16.3 %broadcast_select_fusion.1 = (f32[6144,256]{1,0:T(8,128)S(1)}, f32[6144,256]{1,0:T(8,128)}) fusion(pred[6144]{0:T(1024)(128)(4,1)S(1)} %broadcast_bitcast_fusion.2, f32[6144,256]{0,1:T(8,128)} %copy-done.4, f32[128,256]{1,0:T(8,128)S(1)} %fusion.20, f32[128,256]{1,0:T(8,128)S(1)} %fusion.13, pred[6144]{0:T(1024)(128)(4,1)S(1)} %broadcast_bitcast_fusion.1), kind=kOutput, calls=%fused_computation.24 | convolution fusion | flops 4835049472 | bytes 19148800 | tf_op jit(solution)/shard_map/dot_general | solution.py:29
  1137.0 34.9 %all-reduce.13.cloned.1.call-done = bf16[1536,256]{1,0:T(8,128)(2,1)} async-done(((bf16[1536,256]{1,0:T(8,128)(2,1)}), bf16[1536,256]{1,0:T(8,128)(2,1)}) %all-reduce.13.cloned.1.call-update) | async-done | bytes 786448 | tf_op jit(solution)/shard_map/psum | solution.py:25
  1171.9 40.8 %convolution_subtract_fusion = f32[6144,1536]{0,1:T(8,128)} fusion(f32[6144,256]{1,0:T(8,128)} %copy-done.3, bf16[1536,256]{1,0:T(8,128)(2,1)} %all-reduce.13.cloned.1.call-done, f32[192,8,48,128]{3,2,1,0:T(8,128)} %bitcast.143), kind=kOutput, calls=%fused_computation.13 | convolution fusion | flops 29000466432 | bytes 82575360 | tf_op jit(solution)/shard_map/dot_general | solution.py:29
  1218.0 135.8 %all-reduce.19.cloned.1.call-done = (f32[6144,128]{0,1:T(8,128)}, f32[6144,128]{0,1:T(8,128)}) async-done(((f32[6144,128]{0,1:T(8,128)}, f32[6144,128]{0,1:T(8,128)}), (f32[6144,128]{0,1:T(8,128)}, f32[6144,128]{0,1:T(8,128)})) %all-reduce.19.cloned.1.call-update) | async-done | bytes 6291472 | tf_op jit(solution)/shard_map/psum | solution.py:25
  1360.8 23.4 %all-reduce.15.cloned.1.call-done = f32[256,256]{0,1:T(8,128)} async-done(((f32[256,256]{0,1:T(8,128)}), f32[256,256]{0,1:T(8,128)}) %all-reduce.15.cloned.1.call-update) | async-done | bytes 262160 | tf_op jit(solution)/shard_map/psum | solution.py:133
  1427.0 19.7 %custom-call.20 = f32[2,128,128]{1,2,0:T(8,128)S(1)} custom-call(f32[2,128,128]{2,1,0:T(8,128)S(1)} %get-tuple-element.19), custom_call_target="InvertDiagBlocksLowerTriangular" | custom-call | tf_op jit(solution)/shard_map/jit(_solve_triangular)/triangular_solve | solution.py:135
  1478.7 23.8 %all-reduce.17.cloned.1.call-done = bf16[1536,256]{1,0:T(8,128)(2,1)} async-done(((bf16[1536,256]{1,0:T(8,128)(2,1)}), bf16[1536,256]{1,0:T(8,128)(2,1)}) %all-reduce.17.cloned.1.call-update) | async-done | bytes 786448 | tf_op jit(solution)/shard_map/psum | solution.py:25
  1502.4 35.2 %subtract_bitcast_fusion = f32[1,6144,1536]{1,2,0:T(8,128)} fusion(f32[6144,1536]{0,1:T(8,128)} %convolution_subtract_fusion, f32[6144,256]{1,0:T(8,128)} %copy-done.2, bf16[1536,256]{1,0:T(8,128)(2,1)} %all-reduce.17.cloned.1.call-done), kind=kOutput, calls=%fused_computation.12 | convolution fusion | flops 29000466432 | bytes 82575360 | tf_op jit(solution)/shard_map/dot_general | solution.py:29
  1537.6 36.8 %copy.26 = f32[1,6144,1536]{2,1,0:T(8,128)} copy(f32[1,6144,1536]{1,2,0:T(8,128)} %subtract_bitcast_fusion) | data formatting | bytes 75497472
  (154 shorter events, 225.9 us)
Async XLA Ops:
  7.2 0.7 copy-start
  110.5 346.1 %all-to-all-start = ((bf16[512,128,128]{2,1,0:T(8,128)(2,1)}), bf16[512,128,128]{2,1,0:T(8,128)(2,1)}, u32[]{:S(2)}, u32[]{:S(2)}) async-start(bf16[512,128,128]{2,1,0:T(8,128)(2,1)} %scatter_fusion), calls=%async_computation | async-start | bytes 33554432 | tf_op jit(solution)/shard_map/all_to_all | solution.py:71
  116.8 906.1 %all-reduce.21.cloned.1.call-start = ((), (), s32[]{:S(2)}) async-start(), calls=%async_computation.6 | async-start | bytes 12582912 | tf_op jit(solution)/shard_map/psum | solution.py:25
  468.6 182.0 %collective-permute-start = (bf16[2,4,32,128,128]{4,3,2,1,0:T(8,128)(2,1)}, bf16[2,4,32,128,128]{4,3,2,1,0:T(8,128)(2,1)}, u32[]{:S(2)}, u32[]{:S(2)}) collective-permute-start(bf16[2,4,32,128,128]{4,3,2,1,0:T(8,128)(2,1)} %get-tuple-element.55), channel_id=1, source_target_pairs={{0,16},{16,0},{1,17},{17,1},{2,18},{18,2},{3,19},{19,3},{4,20},{20... | collective-permute-start | bytes 25165832 | tf_op jit(solution)/shard_map/ppermute | solution.py:20
  864.7 188.5 %all-reduce.11.cloned.1.call-start = ((), (), s32[]{:S(2)}) async-start(), calls=%async_computation.1 | async-start | bytes 524288 | tf_op jit(solution)/shard_map/psum | solution.py:133
  1022.9 2.8 copy-start.6
  1026.1 2.7 copy-start.4
  1029.6 142.3 %all-reduce.13.cloned.1.call-start = ((), (), s32[]{:S(2)}) async-start(), calls=%async_computation.2 | async-start | bytes 1572864 | tf_op jit(solution)/shard_map/psum | solution.py:25
  1133.2 2.7 copy-start.3
  1136.9 216.9 %all-reduce.19.cloned.1.call-start = ((), (), s32[]{:S(2)}) async-start(), calls=%async_computation.5 | async-start | bytes 12582912 | tf_op jit(solution)/shard_map/psum | solution.py:25
  1218.0 166.2 %all-reduce.15.cloned.1.call-start = ((), (), s32[]{:S(2)}) async-start(), calls=%async_computation.3 | async-start | bytes 524288 | tf_op jit(solution)/shard_map/psum | solution.py:133
  1353.8 2.8 copy-start.7
  1357.0 2.7 copy-start.5
  1360.4 142.0 %all-reduce.17.cloned.1.call-start = ((), (), s32[]{:S(2)}) async-start(), calls=%async_computation.4 | async-start | bytes 1572864 | tf_op jit(solution)/shard_map/psum | solution.py:25
  1463.9 2.6 copy-start.2
  1537.6 36.8 %copy-start.1 = (s32[2,2,64]{2,1,0:T(2,128)S(1)}, s32[2,2,64]{2,1,0:T(2,128)}, u32[]{:S(2)}) copy-start(s32[2,2,64]{2,1,0:T(2,128)} %param.8) | copy-start | bytes 3076
Sparse Core Ops, SparseCore 0:
  864.8 158.0 all-reduce.20
  1029.7 23.5 all-reduce.10
  1137.0 34.7 all-reduce.12
  1218.1 135.6 all-reduce.18
  1360.6 23.5 all-reduce.14
  1467.6 34.7 all-reduce.16
where the time goes:
time: 1590 us; the launch traced here: 1580 us
  waiting for transfers between devices  794 us (50%)
  local copies, waits for them, and re-layouts  370 us (23%)
  other arithmetic  280 us (18%)
  matrix products  111 us (7%)
  between operations  17.7 us (1%)
    psum x4, waiting for transfers between devices, broadcast(): return lax.psum(block, axis)  353 us
    all_to_all x1, waiting for transfers between devices, per_device(): lax.all_to_all(outgoing, ('row', 'col'), split_axis=0, concat_axis=0, til...  340 us
    unnamed x23, local copies, waits for them, and re-layouts  128 us
    dot_general x4, matrix products, dot_high(): lax.dot_general(left_mat, right_mat, (((1,), (1,)), ((), ())), precision=...  109 us
    scatter-add x1, other arithmetic, per_device(): tile_sums = tile_sums.at[slot_table].add(received.astype(jnp.float32))  104 us
    scatter x1, local copies, waits for them, and re-layouts, per_device(): jnp.zeros((peer_count * capacity, TILE, TILE), jnp.bfloat16).at[placement]  73 us
    another operation x14, other arithmetic, per_device(): lower_f = jnp.linalg.cholesky(diagonal)  69.3 us
    ppermute x1, waiting for transfers between devices, from_partner(): return lax.ppermute(block, axis, route)  54.8 us
  transfers between devices with their start and end apart: 8, of which 8 were waited for; matrix products, arithmetic and copies ran while one was open for 9% of the time, Pallas kernels for 0%

commit v1 on v0

v1 whole, which is shorter than its diff:
```python
import functools

import jax
import jax.numpy as jnp
from jax import lax
from jax.experimental import pallas as pl
from jax.experimental.pallas import tpu as pltpu
from jax.sharding import PartitionSpec as P

TILE = 128
PANELS = 2
PANEL = 256
KT = PANELS * PANEL // TILE
KW = KT * TILE
HI = lax.Precision.HIGHEST
MESH = pl.DeviceIdType.MESH


def pack_kernel(row_count, col_count, cap_cols, group, rows_ref, cols_ref, in_ref, out_ref):
    step = pl.program_id(0)
    for dest_row in range(row_count):
        row = rows_ref[dest_row, step]
        row = pl.multiple_of(row * TILE, TILE)
        for dest_col in range(col_count):
            for slot in range(cap_cols):
                col = pl.multiple_of(cols_ref[dest_col * cap_cols + slot] * TILE, TILE)
                out_ref[dest_row * col_count + dest_col, 0, slot] = in_ref[
                    pl.ds(row, TILE), pl.ds(col, TILE)
                ]


def pack(child, rows, cols, row_count, col_count, cap_rows, cap_cols):
    peers = row_count * col_count
    width = child.shape[1]
    body = functools.partial(pack_kernel, row_count, col_count, cap_cols, 1)

    def wrapped(rows_ref, cols_ref, *refs):
        ins, out_ref = refs[:-1], refs[-1]
        for dest_row in range(row_count):
            for dest_col in range(col_count):
                for slot in range(cap_cols):
                    col = pl.multiple_of(cols_ref[dest_col * cap_cols + slot] * TILE, TILE)
                    out_ref[dest_row * col_count + dest_col, 0, slot] = ins[dest_row][
                        :, pl.ds(col, TILE)
                    ]

    def row_map(dest_row, step, rows_ref, cols_ref):
        return (rows_ref[dest_row, step], 0)

    del body
    return pl.pallas_call(
        wrapped,
        grid_spec=pltpu.PrefetchScalarGridSpec(
            num_scalar_prefetch=2,
            grid=(cap_rows,),
            in_specs=[
                pl.BlockSpec((TILE, width), functools.partial(row_map, dest_row))
                for dest_row in range(row_count)
            ],
            out_specs=pl.BlockSpec(
                (peers, 1, cap_cols, TILE, TILE), lambda step, *_: (0, step, 0, 0, 0)
            ),
        ),
        out_shape=jax.ShapeDtypeStruct((peers, cap_rows, cap_cols, TILE, TILE), child.dtype),
        compiler_params=pltpu.CompilerParams(vmem_limit_bytes=40 * 2**20),
        name="pack_tiles",
    )(rows, cols, *([child] * row_count))


def exchange_kernel(sizes, low, count, has_prior, *refs):
    row_count, col_count, half = sizes
    out_ref = refs[0]
    recv_ref, stage_ref, send_sem, recv_sem, pass_send, pass_recv, own_sem = refs[-7:]
    peers = row_count * col_count
    front = lax.axis_index("front")
    row = lax.axis_index("row")
    col = lax.axis_index("col")
    me = row * col_count + col
    kept = (col // half) == front
    slot = row * half + col % half
    part = pl.ds(low, count)

    barrier = pltpu.get_barrier_semaphore()

    def greet(off, carry):
        dest = (me + off) % peers
        pl.semaphore_signal(
            barrier, inc=1, device_id=(front, dest // col_count, dest % col_count),
            device_id_type=MESH,
        )
        return carry

    lax.fori_loop(1, peers, greet, 0)
    pl.semaphore_signal(barrier, inc=1, device_id=(1 - front, row, col), device_id_type=MESH)
    pl.semaphore_wait(barrier, peers)

    def send(off, target):
        dest = (me + off) % peers
        return pltpu.make_async_remote_copy(
            src_ref=out_ref.at[dest, part],
            dst_ref=target,
            send_sem=send_sem.at[off],
            recv_sem=recv_sem.at[off],
            device_id=(front, dest // col_count, dest % col_count),
            device_id_type=MESH,
        )

    def forward(source, where):
        return pltpu.make_async_remote_copy(
            src_ref=source,
            dst_ref=recv_ref.at[1, where, part],
            send_sem=pass_send.at[where],
            recv_sem=pass_recv.at[where],
            device_id=(1 - front, row, col),
            device_id_type=MESH,
        )

    own = pltpu.make_async_copy(out_ref.at[me, part], recv_ref.at[0, slot, part], own_sem)

    @pl.when(kept)
    def _():
        def start(off, carry):
            send(off, recv_ref.at[0, slot, part]).start()
            return carry

        lax.fori_loop(1, peers, start, 0)
        own.start()

    @pl.when(jnp.logical_not(kept))
    def _():
        def start(off, carry):
            send(off, stage_ref.at[slot]).start()
            return carry

        lax.fori_loop(1, peers, start, 0)
        forward(out_ref.at[me, part], slot).start()

    def relay(off, carry):
        source = (me + peers - off) % peers
        source_col = source % col_count
        where = (source // col_count) * half + source_col % half

        @pl.when((source_col // half) != front)
        def _():
            send(off, stage_ref.at[where]).wait_recv()
            forward(stage_ref.at[where], where).start()

        return carry

    lax.fori_loop(1, peers, relay, 0)

    def finish(off, carry):
        source = (me + peers - off) % peers
        source_col = source % col_count
        where = (source // col_count) * half + source_col % half

        @pl.when((source_col // half) == front)
        def _():
            send(off, recv_ref.at[0, where, part]).wait_recv()

        send(off, stage_ref.at[slot]).wait_send()
        return carry

    lax.fori_loop(1, peers, finish, 0)

    @pl.when(kept)
    def _():
        own.wait()

    def close(where, carry):
        forward(stage_ref.at[where], where).wait_send()
        forward(stage_ref.at[where], where).wait_recv()
        return carry

    lax.fori_loop(0, row_count * half, close, 0)


def exchange(outgoing, prior, token, sizes, low, count, number):
    row_count, col_count, half = sizes
    peers = row_count * col_count
    slots = row_count * half
    cap_rows, cap_cols = outgoing.shape[1:3]
    anywhere = pl.BlockSpec(memory_space=pl.ANY)
    operands = [outgoing]
    aliases = {}
    if prior is not None:
        operands += [token, prior]
        aliases = {2: 0}
    recv, _ = pl.pallas_call(
        functools.partial(exchange_kernel, sizes, low, count, prior is not None),
        out_shape=(
            jax.ShapeDtypeStruct((2, slots, cap_rows, cap_cols, TILE, TILE), outgoing.dtype),
            jax.ShapeDtypeStruct((slots, count, cap_cols, TILE, TILE), outgoing.dtype),
        ),
        in_specs=[anywhere] * len(operands),
        out_specs=(anywhere, anywhere),
        scratch_shapes=[
            pltpu.SemaphoreType.DMA((peers,)),
            pltpu.SemaphoreType.DMA((peers,)),
            pltpu.SemaphoreType.DMA((slots,)),
            pltpu.SemaphoreType.DMA((slots,)),
            pltpu.SemaphoreType.DMA,
        ],
        input_output_aliases=aliases,
        compiler_params=pltpu.CompilerParams(collective_id=number, has_side_effects=True),
        name="exchange_tiles_%d" % number,
    )(*operands)
    return recv


def combine_kernel(rows_at, local_ct, cap_cols, update, place_ref, cols_ref, *refs):
    step = pl.program_id(0)
    tiles = refs[: 2 * rows_at]
    front_ref = refs[2 * rows_at]
    out_ref = refs[-1]
    for at in range(rows_at):
        span = pl.ds(at * TILE, TILE)
        for ct in range(local_ct):
            lanes = pl.ds(ct * TILE, TILE)
            total = front_ref[0, span, lanes].astype(jnp.float32)
            for sib in range(2):
                where = cols_ref[sib, ct]
                there = (place_ref[3, sib, step * rows_at + at] > 0) & (where >= 0)
                where = jnp.maximum(where, 0)
                tile = tiles[2 * at + sib][0, where // cap_cols, 0, where % cap_cols]
                total = total + jnp.where(there, tile.astype(jnp.float32), 0.0)
            out_ref[0, span, lanes] = total
    if update:
        left_ref, right_ref = refs[2 * rows_at + 1 : 2 * rows_at + 3]
        for ct in range(0, local_ct, 2):
            lanes = pl.ds(ct * TILE, 2 * TILE)
            out_ref[0, :, lanes] -= lax.dot_general(
                left_ref[...], right_ref[:, lanes], (((1,), (0,)), ((), ())),
                preferred_element_type=jnp.float32,
            )


def combine(recv, front_block, place, cols, sizes, row_tiles, rows_at, factors):
    row_count, col_count, half = sizes
    quarter = half // 2
    cap_rows, cap_cols = recv.shape[2:4]
    width = front_block.shape[2]
    local_ct = width // TILE

    def tile_map(at, sib, step, place_ref, cols_ref):
        tile = step * rows_at + at
        return (place_ref[0, sib, tile], place_ref[1, sib, tile], place_ref[2, sib, tile], 0, 0, 0)

    recv = recv.reshape(2, row_count * 2, quarter, cap_rows, cap_cols, TILE, TILE)
    recv = recv.reshape(4 * row_count, quarter, cap_rows, cap_cols, TILE, TILE)

    def block_map(at, sib, step, place_ref, cols_ref):
        tile = step * rows_at + at
        return (place_ref[0, sib, tile], 0, place_ref[1, sib, tile], 0, 0, 0)

    in_specs = []
    for at in range(rows_at):
        for sib in range(2):
            in_specs.append(
                pl.BlockSpec(
                    (1, quarter, 1, cap_cols, TILE, TILE), functools.partial(block_map, at, sib)
                )
            )
    in_specs.append(pl.BlockSpec((1, rows_at * TILE, width), lambda step, *_: (0, step, 0)))
    operands = [recv] * (2 * rows_at) + [front_block]
    if factors is not None:
        in_specs.append(pl.BlockSpec((rows_at * TILE, KW), lambda step, *_: (step, 0)))
        in_specs.append(pl.BlockSpec((KW, width), lambda step, *_: (0, 0)))
        operands += list(factors)
    return pl.pallas_call(
        functools.partial(combine_kernel, rows_at, local_ct, cap_cols, factors is not None),
        grid_spec=pltpu.PrefetchScalarGridSpec(
            num_scalar_prefetch=2,
            grid=(row_tiles // rows_at,),
            in_specs=in_specs,
            out_specs=pl.BlockSpec((1, rows_at * TILE, width), lambda step, *_: (0, step, 0)),
        ),
        out_shape=jax.ShapeDtypeStruct((1, row_tiles * TILE, width), jnp.float32),
        compiler_params=pltpu.CompilerParams(vmem_limit_bytes=48 * 2**20),
        name="combine_update" if factors is not None else "combine_pivot_rows",
    )(place, cols, *operands)


def per_device(front_orig, child_update, tile_map):
    row_count = lax.axis_size("row")
    col_count = lax.axis_size("col")
    front_id = lax.axis_index("front")
    row_id = lax.axis_index("row")
    col_id = lax.axis_index("col")
    local_rt = front_orig.shape[1] // TILE
    local_ct = front_orig.shape[2] // TILE
    band_rows = child_update.shape[0] // TILE
    band_cols = child_update.shape[1] // TILE
    nct = tile_map.shape[2]
    cap_rows = max(1, band_rows // row_count)
    cap_cols = max(1, band_cols // col_count)
    half = col_count // 2
    quarter = col_count // 4
    ratio = col_count // row_count
    sizes = (row_count, col_count, half)
    pivot_tiles = max(1, KT // row_count)

    every = jnp.arange(nct)
    band_of = every // band_rows
    same = (band_of[:, None] == band_of[None, :]) & (
        tile_map[..., :, None] % row_count == tile_map[..., None, :] % row_count
    )
    before = same & (tile_map[..., None, :] < tile_map[..., :, None])
    rank = jnp.sum(before.astype(jnp.int32), axis=-1)

    child_no = col_id // quarter
    sender_map = tile_map[child_no // 2, child_no % 2]
    sender_rank = rank[child_no // 2, child_no % 2]
    first = (front_id * row_count + row_id) * band_rows
    band_map = lax.dynamic_slice(sender_map, (first,), (band_rows,))
    band_rank = lax.dynamic_slice(sender_rank, (first,), (band_rows,))
    wanted = jnp.arange(row_count * cap_rows)[:, None]
    rows = jnp.sum(
        jnp.where(
            (band_map % row_count * cap_rows + band_rank)[None, :] == wanted,
            jnp.arange(band_rows)[None, :],
            0,
        ),
        axis=1,
    ).reshape(row_count, cap_rows)
    col_map = lax.dynamic_slice(sender_map, (col_id % quarter * band_cols,), (band_cols,))
    wanted = jnp.arange(col_count * cap_cols)[:, None]
    cols = jnp.sum(
        jnp.where(
            (col_map % col_count * cap_cols + jnp.arange(band_cols) // col_count)[None, :]
            == wanted,
            jnp.arange(band_cols)[None, :],
            0,
        ),
        axis=1,
    )
    outgoing = pack(
        child_update, rows.astype(jnp.int32), cols.astype(jnp.int32),
        row_count, col_count, cap_rows, cap_cols,
    )

    own_maps = lax.dynamic_index_in_dim(tile_map, front_id, 0, keepdims=False)
    own_rank = lax.dynamic_index_in_dim(rank, front_id, 0, keepdims=False)
    row_tile = row_id + row_count * jnp.arange(local_rt)
    hit = own_maps[:, None, :] == row_tile[None, :, None]
    source = (every // band_rows)[None, None, :]
    side = jnp.where(source // row_count == front_id, 0, 1)
    sib_no = jnp.arange(2)[:, None, None]
    chunk = (side * row_count + source % row_count) * 2 + sib_no

    def choose(values):
        return jnp.sum(jnp.where(hit, values, 0), axis=-1)

    place = jnp.stack(
        [
            choose(chunk),
            choose(own_rank[:, None, :]),
            jnp.zeros((2, local_rt), jnp.int32),
            choose(1),
        ]
    ).astype(jnp.int32)
    col_tile = col_id + col_count * jnp.arange(local_ct)
    col_hit = own_maps[:, None, :] == col_tile[None, :, None]
    col_place = every // band_cols * cap_cols + every % band_cols // col_count
    col_where = jnp.sum(jnp.where(col_hit, col_place + 1, 0), axis=-1).astype(jnp.int32) - 1

    early = min(pivot_tiles, cap_rows)
    recv = exchange(outgoing, None, None, sizes, 0, early, 1)
    pivot_rows = combine(
        recv, front_orig, place, col_where, sizes, pivot_tiles, 1, None
    )[0]
    gathered = lax.all_gather(pivot_rows.reshape(pivot_tiles, TILE, -1), "row", axis=0)
    gathered = gathered.swapaxes(0, 1).reshape(row_count * pivot_tiles * TILE, -1)[:KW]
    corner = lax.all_gather(gathered[:, :TILE], "col", axis=0)[:KT]
    diagonal = corner.swapaxes(0, 1).reshape(KW, KW)

    if early < cap_rows:
        middle = (cap_rows - early) // 2
        recv = exchange(outgoing, recv, pivot_rows, sizes, early, middle, 2)

    eye = jnp.eye(PANEL, dtype=jnp.float32)
    dot = functools.partial(jnp.dot, precision=HI, preferred_element_type=jnp.float32)
    low0 = jnp.linalg.cholesky(diagonal[:PANEL, :PANEL])
    inv0 = jax.scipy.linalg.solve_triangular(low0, eye, lower=True)
    g10 = dot(diagonal[PANEL:, :PANEL], inv0.T)
    low1 = jnp.linalg.cholesky(diagonal[PANEL:, PANEL:] - dot(g10, g10.T))
    inv1 = jax.scipy.linalg.solve_triangular(low1, eye, lower=True)

    g0 = dot(inv0, gathered[:PANEL])
    g1 = dot(inv1, gathered[PANEL:] - dot(g10, g0))
    col_tiles = jnp.repeat(col_tile, TILE)
    g1 = jnp.where((col_tiles >= 2)[None, :], g1, 0.0)
    mine = jnp.concatenate([g0, g1], axis=0).T
    trail0 = jnp.where((col_tiles >= 2)[None, :], g0, 0.0)
    trail1 = jnp.where((col_tiles >= 4)[None, :], g1, 0.0)
    right = jnp.concatenate([trail0, trail1], axis=0).astype(jnp.bfloat16)

    groups = [[q * row_count + h for h in range(row_count)] for q in range(ratio)]
    share = mine.reshape(row_count, local_ct * TILE // row_count, KW)
    share = lax.all_to_all(
        share, "col", split_axis=0, concat_axis=0, axis_index_groups=groups, tiled=True
    )
    share = lax.dynamic_index_in_dim(share, row_id, 0, keepdims=False)
    whole = lax.all_gather(share, "col", axis=0)

    if early < cap_rows:
        recv = exchange(outgoing, recv, share, sizes, early + middle, cap_rows - early - middle, 3)

    factor = (
        whole.reshape(ratio, local_ct, TILE, KW).swapaxes(0, 1).reshape(local_rt * TILE, KW)
    )
    row_tiles = jnp.repeat(row_tile, TILE)[:, None]
    panel_of = jnp.arange(KW)[None, :] // PANEL
    left = jnp.where(row_tiles >= 2 * panel_of + 2, factor, 0.0).astype(jnp.bfloat16)
    front = combine(recv, front_orig, place, col_where, sizes, local_rt, 2, (left, right))
    return (front, factor[None])


def solution(mesh):
    placed = (P("front", "row", "col"), P(("front", "row"), "col"), P())
    return jax.shard_map(
        per_device,
        mesh=mesh,
        in_specs=placed,
        out_specs=(P("front", "row", "col"), P("front", "row", None)),
        check_vma=False,
    )
```

time: 1590 us -> 935 us (0.59)
  waiting for transfers between devices: 794 us -> 70.3 us
  Pallas kernels: 0 us -> 610 us
  local copies, waits for them, and re-layouts: 370 us -> 54.2 us
  other arithmetic: 280 us -> 138 us
  matrix products: 111 us -> 24 us
    pallas_call x0 -> x6, Pallas kernels: none -> 610 us  [the longest x3 551 us: exchange(): pl.pallas_call(functools.partial(exchange_kernel, sizes, low, count, prio...]
    psum x6 -> x0, waiting for transfers between devices: 399 us -> none  [the longest x4 353 us: broadcast(): return lax.psum(block, axis)]
    all_to_all x1 -> x0, waiting for transfers between devices: 340 us -> none  [per_device(): lax.all_to_all(outgoing, ('row', 'col'), split_axis=0, concat_axis=0, til...]
    unnamed x23 -> x16, local copies, waits for them, and re-layouts: 128 us -> 2.05 us
    scatter-add x1 -> x0, other arithmetic: 104 us -> none  [per_device(): tile_sums = tile_sums.at[slot_table].add(received.astype(jnp.float32))]
    scatter x2 -> x0, local copies, waits for them, and re-layouts: 104 us -> none  [the longest x1 73 us: per_device(): jnp.zeros((peer_count * capacity, TILE, TILE), jnp.bfloat16).at[placement]]
    dot_general x4 -> x5, matrix products: 109 us -> 10.8 us  [the longest x2 3.88 us: per_device(): g1 = dot(inv1, gathered[PANEL:] - dot(g10, g0))]
    all_gather x0 -> x3, waiting for transfers between devices: none -> 70.3 us  [the longest x1 44.5 us: per_device(): lax.all_gather(pivot_rows.reshape(pivot_tiles, TILE, -1), 'row', axis=0)]
  transfers between devices with their start and end apart: 8 -> 3, of which waited for: 8 -> 2; matrix products, arithmetic and copies ran while one was open for 9% -> 0% of each run, Pallas kernels for 0% -> 47%
where the time goes in v1:
time: 935 us; the launch traced here: 922 us
  Pallas kernels  610 us (65%)
  other arithmetic  138 us (15%)
  waiting for transfers between devices  70.3 us (8%)
  local copies, waits for them, and re-layouts  54.2 us (6%)
  matrix products  24 us (3%)
  between operations  16.8 us (2%)
    pallas_call x3, Pallas kernels, exchange(): pl.pallas_call(functools.partial(exchange_kernel, sizes, low, count, prio...  551 us
    all_gather x1, waiting for transfers between devices, per_device(): lax.all_gather(pivot_rows.reshape(pivot_tiles, TILE, -1), 'row', axis=0)  44.5 us
    pallas_call x2, Pallas kernels, combine(): pl.pallas_call(functools.partial(combine_kernel, rows_at, local_ct, cap_c...  43.4 us
    another operation x7, other arithmetic, per_device(): low1 = jnp.linalg.cholesky(diagonal[PANEL:, PANEL:] - dot(g10, g10.T))  41.9 us
    another operation x7, other arithmetic, per_device(): low0 = jnp.linalg.cholesky(diagonal[:PANEL, :PANEL])  35.9 us
    all_gather x1, waiting for transfers between devices, per_device(): corner = lax.all_gather(gathered[:, :TILE], 'col', axis=0)[:KT]  25.8 us
    another operation x3, other arithmetic, per_device(): inv0 = jax.scipy.linalg.solve_triangular(low0, eye, lower=True)  22.8 us
    another operation x2, other arithmetic, per_device(): inv1 = jax.scipy.linalg.solve_triangular(low1, eye, lower=True)  22.8 us
  transfers between devices with their start and end apart: 3, of which 2 were waited for; matrix products, arithmetic and copies ran while one was open for 0% of the time, Pallas kernels for 47%

profile of v1, /device:TPU:25, one launch (start us, length us, event | category | flops | bytes accessed | tf_op | source)
XLA Modules:
  0.0 921.7 jit_solution(5382589877838666896)
XLA Ops:
  12.2 15.6 %pack_tiles.1.refs_0_ = bf16[16,8,4,128,128]{4,3,2,1,0:T(8,128)(2,1)} custom-call(s32[2,8]{1,0:T(2,128)S(1)} %reshape.340.rows_ref, s32[32]{0:T(128)S(1)} %select_reduce_fusion.4.cols_ref, bf16[2048,4096]{1,0:T(8,128)(2,1)} %refs_1_.1, bf16[2048,4096]{1,0:T(8,128)(2,1)} %refs_1_.1), custom_call_target="tpu_custom_call" | custom-call | tf_op jit(solution)/shard_map/pack_tiles/pallas_call | solution.py:51
  27.8 115.3 %exchange_tiles_1.1 = (bf16[2,8,8,4,128,128]{5,4,3,2,1,0:T(8,128)(2,1)}, bf16[8,2,4,128,128]{4,3,2,1,0:T(8,128)(2,1)}) custom-call(bf16[16,8,4,128,128]{4,3,2,1,0:T(8,128)(2,1)} %pack_tiles.1.refs_0_), custom_call_target="tpu_custom_call" | custom-call | tf_op jit(solution)/shard_map/exchange_tiles_1/pallas_call | solution.py:189
  143.4 3.2 combine_pivot_rows.1
  146.7 44.5 %all-gather.5.cloned.1.call-done = f32[2,2,128,1536]{3,2,0,1:T(8,128)} async-done(((f32[1,2,128,1536]{3,2,0,1:T(8,128)}), f32[2,2,128,1536]{3,2,0,1:T(8,128)}) %all-gather.5.cloned.1.call-update) | async-done | bytes 3145744 | tf_op jit(solution)/shard_map/all_gather | solution.py:372
  195.7 25.8 %all-gather.9.cloned.1.call-done = f32[4096,128]{1,0:T(8,128)} async-done(((f32[512,128]{1,0:T(8,128)}), f32[4096,128]{1,0:T(8,128)}) %all-gather.9.cloned.1.call-update) | async-done | bytes 2097168 | tf_op jit(solution)/shard_map/all_gather | solution.py:374
  231.6 11.7 %cholesky.130 = f32[128,128]{1,0:T(8,128)S(1)} custom-call(f32[128,128]{1,0:T(8,128)S(1)} %cholesky.194), custom_call_target="Cholesky" | custom-call | tf_op jit(solution)/shard_map/jit(cholesky)/cholesky | solution.py:383
  244.1 10.4 %custom-call.13 = f32[1,128,128]{1,2,0:T(8,128)} custom-call(f32[1,128,128]{2,1,0:T(8,128)S(1)} %get-tuple-element.58), custom_call_target="InvertDiagBlocksLowerTriangular" | custom-call | tf_op jit(solution)/shard_map/jit(cholesky)/cholesky | solution.py:383
  258.0 11.7 %cholesky.147 = f32[128,128]{1,0:T(8,128)S(1)} custom-call(f32[128,128]{1,0:T(8,128)S(1)} %convolution_subtract_fusion.5), custom_call_target="Cholesky" | custom-call | tf_op jit(solution)/shard_map/jit(cholesky)/cholesky | solution.py:383
  275.3 7.1 while.4
  282.4 20.6 %custom-call.14 = f32[2,128,128]{1,2,0:T(8,128)} custom-call(f32[2,128,128]{2,1,0:T(8,128)S(1)} %get-tuple-element.24), custom_call_target="InvertDiagBlocksLowerTriangular" | custom-call | tf_op jit(solution)/shard_map/jit(_solve_triangular)/triangular_solve | solution.py:384
  314.9 13.2 %cholesky.164 = f32[128,128]{1,0:T(8,128)} custom-call(f32[128,128]{1,0:T(8,128)} %cholesky.197), custom_call_target="Cholesky" | custom-call | tf_op jit(solution)/shard_map/jit(cholesky)/cholesky | solution.py:386
  330.2 11.3 %custom-call.15 = f32[1,128,128]{1,2,0:T(8,128)} custom-call(f32[1,128,128]{2,1,0:T(8,128)} %get-tuple-element.54), custom_call_target="InvertDiagBlocksLowerTriangular" | custom-call | tf_op jit(solution)/shard_map/jit(cholesky)/cholesky | solution.py:386
  346.5 13.2 %cholesky.181 = f32[128,128]{1,0:T(8,128)} custom-call(f32[128,128]{1,0:T(8,128)} %convolution_subtract_fusion.4), custom_call_target="Cholesky" | custom-call | tf_op jit(solution)/shard_map/jit(cholesky)/cholesky | solution.py:386
  365.3 8.5 while.5
  366.8 2.9 bitcast_dynamic-update-slice_fusion.5
  371.0 2.8 bitcast_dynamic-update-slice_fusion.5
  373.8 21.1 %custom-call.16 = f32[2,128,128]{1,2,0:T(8,128)} custom-call(f32[2,128,128]{2,1,0:T(8,128)} %get-tuple-element.25), custom_call_target="InvertDiagBlocksLowerTriangular" | custom-call | tf_op jit(solution)/shard_map/jit(_solve_triangular)/triangular_solve | solution.py:387
  398.5 3.3 select_convert_fusion.1
  408.2 7.4 all_to_all.5
  417.0 269.7 %exchange_tiles_2.1 = (bf16[2,8,8,4,128,128]{5,4,3,2,1,0:T(8,128)(2,1)}, bf16[8,3,4,128,128]{4,3,2,1,0:T(8,128)(2,1)}) custom-call(bf16[16,8,4,128,128]{4,3,2,1,0:T(8,128)(2,1)} %pack_tiles.1.refs_0_, f32[256,1536]{1,0:T(8,128)} %bitcast.32.refs_1_, bf16[2,8,8,4,128,128]{5,4,3,2,1,0:T(8,128)(2,1)} %get-tuple-element.7.refs_2_), custom_call_target="tpu_custom_call", output_to_operand_aliasing={{0}: (2, {})} | custom-call | tf_op jit(solution)/shard_map/exchange_tiles_2/pallas_call | solution.py:189
  688.1 166.3 %exchange_tiles_3.1 = (bf16[2,8,8,4,128,128]{5,4,3,2,1,0:T(8,128)(2,1)}, bf16[8,3,4,128,128]{4,3,2,1,0:T(8,128)(2,1)}) custom-call(bf16[16,8,4,128,128]{4,3,2,1,0:T(8,128)(2,1)} %pack_tiles.1.refs_0_, f32[768,512]{1,0:T(8,128)} %fusion.68.refs_1_, bf16[2,8,8,4,128,128]{5,4,3,2,1,0:T(8,128)(2,1)} %get-tuple-element.8.refs_2_), custom_call_target="tpu_custom_call", output_to_operand_aliasing={{0}: (2, {})} | custom-call | tf_op jit(solution)/shard_map/exchange_tiles_3/pallas_call | solution.py:189
  854.6 12.0 %copy.42 = f32[12,4,128,512]{3,2,1,0:T(8,128)} copy(f32[12,4,128,512]{3,2,0,1:T(8,128)} %bitcast.123) | data formatting | bytes 25165824 | tf_op jit(solution)/shard_map/transpose | solution.py:410
  866.6 8.3 fusion.refs_5_
  874.8 40.2 %combine_update.1 = f32[1,6144,1536]{2,1,0:T(8,128)} custom-call(s32[4,2,48]{2,1,0:T(2,128)S(1)} %pad_add_fusion.place_ref, s32[2,12]{1,0:T(2,128)S(1)} %broadcast_add_fusion.cols_ref, bf16[8,2,8,4,128,128]{5,4,3,2,1,0:T(8,128)(2,1)} %bitcast.118, bf16[8,2,8,4,128,128]{5,4,3,2,1,0:T(8,128)(2,1)} %bitcast.119, bf16[8,2,8,4,128,128]{5,4,3,2,1,0:T(8,128)(2,1)} %bitcast.120, ...), custom_call_target="tpu_custom_call" | custom-call | tf_op jit(solution)/shard_map/combine_update/pallas_call | solution.py:270
  (106 shorter events, 74.4 us)
Async XLA Ops:
  7.2 184.0 %all-gather.5.cloned.1.call-start = ((), (), s32[]{:S(2)}) async-start(), calls=%async_computation.1 | async-start | bytes 4718592 | tf_op jit(solution)/shard_map/all_gather | solution.py:372
  7.3 135.8 %copy-start.6 = (s32[48]{0:T(128)}, s32[48]{0:T(128)S(1)}, u32[]{:S(2)}) copy-start(s32[48]{0:T(128)S(1)} %multiply_add_fusion.1) | copy-start | bytes 580
  146.7 74.8 %all-gather.9.cloned.1.call-start = ((), (), s32[]{:S(2)}) async-start(), calls=%async_computation.3 | async-start | bytes 2359296 | tf_op jit(solution)/shard_map/all_gather | solution.py:374
  192.9 661.7 %all-gather.7.cloned.1.call-start = ((), (), s32[]{:S(2)}) async-start(), calls=%async_computation.2 | async-start | bytes 14155776 | tf_op jit(solution)/shard_map/all_gather | solution.py:404
  193.5 110.7 %copy-start.2 = (f32[256,256]{1,0:T(8,128)}, f32[256,256]{1,0:T(8,128)S(1)}, u32[]{:S(2)}) copy-start(f32[256,256]{1,0:T(8,128)S(1)} %fusion.8) | copy-start | bytes 786436
  230.9 0.7 copy-start.5
  306.5 0.6 copy-start.3
  313.6 0.7 copy-start.4
  417.0 269.7 %copy-start.7 = (s32[48]{0:T(128)S(1)}, s32[48]{0:T(128)}, u32[]{:S(2)}) copy-start(s32[48]{0:T(128)} %copy-done.6) | copy-start | bytes 580
  688.1 166.3 %copy-start = (bf16[256,1536]{1,0:T(8,128)(2,1)S(1)}, bf16[256,1536]{1,0:T(8,128)(2,1)}, u32[]{:S(2)}) copy-start(bf16[256,1536]{1,0:T(8,128)(2,1)} %get-tuple-element.63) | copy-start | bytes 2359300
  688.1 166.4 %copy-start.1 = (bf16[256,1536]{1,0:T(8,128)(2,1)S(1)}, bf16[256,1536]{1,0:T(8,128)(2,1)}, u32[]{:S(2)}) copy-start(bf16[256,1536]{1,0:T(8,128)(2,1)} %get-tuple-element.65) | copy-start | bytes 2359300
Sparse Core Ops, SparseCore 0:
  146.8 44.3 all-gather.4
  193.4 28.1 all-gather.8
  417.1 232.9 all-gather.6

commit v2 on v1

--- a/solution.py
+++ b/solution.py
@@ -16,25 +16,11 @@
 MESH = pl.DeviceIdType.MESH
 
 
-def pack_kernel(row_count, col_count, cap_cols, group, rows_ref, cols_ref, in_ref, out_ref):
-    step = pl.program_id(0)
-    for dest_row in range(row_count):
-        row = rows_ref[dest_row, step]
-        row = pl.multiple_of(row * TILE, TILE)
-        for dest_col in range(col_count):
-            for slot in range(cap_cols):
-                col = pl.multiple_of(cols_ref[dest_col * cap_cols + slot] * TILE, TILE)
-                out_ref[dest_row * col_count + dest_col, 0, slot] = in_ref[
-                    pl.ds(row, TILE), pl.ds(col, TILE)
-                ]
-
-
 def pack(child, rows, cols, row_count, col_count, cap_rows, cap_cols):
     peers = row_count * col_count
     width = child.shape[1]
-    body = functools.partial(pack_kernel, row_count, col_count, cap_cols, 1)
-
-    def wrapped(rows_ref, cols_ref, *refs):
+
+    def body(rows_ref, cols_ref, *refs):
         ins, out_ref = refs[:-1], refs[-1]
         for dest_row in range(row_count):
             for dest_col in range(col_count):
@@ -47,9 +33,8 @@
     def row_map(dest_row, step, rows_ref, cols_ref):
         return (rows_ref[dest_row, step], 0)
 
-    del body
     return pl.pallas_call(
-        wrapped,
+        body,
         grid_spec=pltpu.PrefetchScalarGridSpec(
             num_scalar_prefetch=2,
             grid=(cap_rows,),
@@ -67,10 +52,71 @@
     )(rows, cols, *([child] * row_count))
 
 
-def exchange_kernel(sizes, low, count, has_prior, *refs):
+def invert_factor(diag_ref, inv_ref, work_ref, small_ref, between):
+    blocks = KW // TILE
+    rows_of = lax.broadcasted_iota(jnp.int32, (KW, KW), 0)
+    cols_of = lax.broadcasted_iota(jnp.int32, (KW, KW), 1)
+    work_ref[:, :KW] = diag_ref[...]
+    work_ref[:, KW:] = jnp.where(rows_of == cols_of, 1.0, 0.0)
+    row_no = lax.broadcasted_iota(jnp.int32, (TILE, 1), 0)
+    lane_no = lax.broadcasted_iota(jnp.int32, (1, TILE), 1)
+    small_rows = lax.broadcasted_iota(jnp.int32, (TILE, TILE), 0)
+    small_cols = lax.broadcasted_iota(jnp.int32, (TILE, TILE), 1)
+    for block in range(blocks):
+        span = pl.ds(block * TILE, TILE)
+        small_ref[:, :TILE] = work_ref[span, span]
+        small_ref[:, TILE:] = jnp.where(small_rows == small_cols, 1.0, 0.0)
+
+        def step(k, carry):
+            pivot_row = small_ref[pl.ds(k, 1), :]
+            here = lane_no == k
+            pivot = jnp.sum(jnp.where(here, pivot_row[:, :TILE], 0.0), axis=1, keepdims=True)
+            scale = 1.0 / jnp.sqrt(pivot)
+            column = jnp.sum(jnp.where(here, small_ref[:, :TILE], 0.0), axis=1, keepdims=True)
+            scaled = pivot_row * scale
+            times = jnp.where(row_no > k, column * scale, 0.0)
+            small_ref[...] = jnp.where(row_no == k, scaled, small_ref[...] - times * scaled)
+            return carry
+
+        lax.fori_loop(0, TILE, step, 0)
+        reduced = jnp.dot(
+            small_ref[:, TILE:], work_ref[span, :], precision=HI,
+            preferred_element_type=jnp.float32,
+        )
+        work_ref[span, :] = reduced
+        if block + 1 < blocks:
+            rest = pl.ds((block + 1) * TILE, KW - (block + 1) * TILE)
+            work_ref[rest, :] -= lax.dot_general(
+                work_ref[span, rest], work_ref[span, :], (((0,), (0,)), ((), ())),
+                precision=HI, preferred_element_type=jnp.float32,
+            )
+        between(block)
+    inv_ref[...] = jnp.where(rows_of >= cols_of, work_ref[:, KW:], 0.0)
+
+
+def factor_alone(diagonal):
+    def body(diag_ref, inv_ref, work_ref, small_ref):
+        invert_factor(diag_ref, inv_ref, work_ref, small_ref, lambda block: None)
+
+    return pl.pallas_call(
+        body,
+        out_shape=jax.ShapeDtypeStruct((KW, KW), jnp.float32),
+        scratch_shapes=[
+            pltpu.VMEM((KW, 2 * KW), jnp.float32),
+            pltpu.VMEM((TILE, 2 * TILE), jnp.float32),
+        ],
+        compiler_params=pltpu.CompilerParams(vmem_limit_bytes=32 * 2**20),
+        name="factor_inverse",
+    )(diagonal)
+
+
+def exchange_kernel(sizes, low, count, inputs, factoring, *refs):
     row_count, col_count, half = sizes
     out_ref = refs[0]
-    recv_ref, stage_ref, send_sem, recv_sem, pass_send, pass_recv, own_sem = refs[-7:]
+    recv_ref, stage_ref = refs[inputs : inputs + 2]
+    if factoring:
+        inv_ref, work_ref, small_ref = refs[inputs + 2], refs[-7], refs[-6]
+    send_sem, recv_sem, pass_send, pass_recv, own_sem = refs[-5:]
     peers = row_count * col_count
     front = lax.axis_index("front")
     row = lax.axis_index("row")
@@ -147,7 +193,16 @@
 
         return carry
 
-    lax.fori_loop(1, peers, relay, 0)
+    if factoring:
+        parts = KW // TILE
+        cuts = [1 + (peers - 1) * at // parts for at in range(parts + 1)]
+
+        def between(block):
+            lax.fori_loop(cuts[block], cuts[block + 1], relay, 0)
+
+        invert_factor(refs[1], inv_ref, work_ref, small_ref, between)
+    else:
+        lax.fori_loop(1, peers, relay, 0)
 
     def finish(off, carry):
         source = (me + peers - off) % peers
@@ -175,26 +230,46 @@
     lax.fori_loop(0, row_count * half, close, 0)
 
 
-def exchange(outgoing, prior, token, sizes, low, count, number):
+def exchange(outgoing, prior, diagonal, tokens, sizes, low, count, number):
     row_count, col_count, half = sizes
     peers = row_count * col_count
     slots = row_count * half
     cap_rows, cap_cols = outgoing.shape[1:3]
     anywhere = pl.BlockSpec(memory_space=pl.ANY)
-    operands = [outgoing]
+    vmem = pl.BlockSpec(memory_space=pltpu.VMEM)
+    factoring = diagonal is not None
+    operands, in_specs = [outgoing], [anywhere]
+    if factoring:
+        operands.append(diagonal)
+        in_specs.append(vmem)
+    operands += tokens
+    in_specs += [anywhere] * len(tokens)
     aliases = {}
     if prior is not None:
-        operands += [token, prior]
-        aliases = {2: 0}
-    recv, _ = pl.pallas_call(
-        functools.partial(exchange_kernel, sizes, low, count, prior is not None),
-        out_shape=(
-            jax.ShapeDtypeStruct((2, slots, cap_rows, cap_cols, TILE, TILE), outgoing.dtype),
-            jax.ShapeDtypeStruct((slots, count, cap_cols, TILE, TILE), outgoing.dtype),
-        ),
-        in_specs=[anywhere] * len(operands),
-        out_specs=(anywhere, anywhere),
-        scratch_shapes=[
+        aliases = {len(operands): 0}
+        operands.append(prior)
+        in_specs.append(anywhere)
+    out_shape = [
+        jax.ShapeDtypeStruct((2, slots, cap_rows, cap_cols, TILE, TILE), outgoing.dtype),
+        jax.ShapeDtypeStruct((slots, count, cap_cols, TILE, TILE), outgoing.dtype),
+    ]
+    out_specs = [anywhere, anywhere]
+    scratch = []
+    if factoring:
+        out_shape.append(jax.ShapeDtypeStruct((KW, KW), jnp.float32))
+        out_specs.append(vmem)
+        scratch = [
+            pltpu.VMEM((KW, 2 * KW), jnp.float32),
+            pltpu.VMEM((TILE, 2 * TILE), jnp.float32),
+        ]
+    sent = peers * count * cap_cols * TILE * TILE * 2
+    return pl.pallas_call(
+        functools.partial(exchange_kernel, sizes, low, count, len(operands), factoring),
+        out_shape=out_shape,
+        in_specs=in_specs,
+        out_specs=out_specs,
+        scratch_shapes=scratch
+        + [
             pltpu.SemaphoreType.DMA((peers,)),
             pltpu.SemaphoreType.DMA((peers,)),
             pltpu.SemaphoreType.DMA((slots,)),
@@ -202,17 +277,19 @@
             pltpu.SemaphoreType.DMA,
         ],
         input_output_aliases=aliases,
-        compiler_params=pltpu.CompilerParams(collective_id=number, has_side_effects=True),
+        compiler_params=pltpu.CompilerParams(
+            collective_id=number, has_side_effects=True, vmem_limit_bytes=56 * 2**20
+        ),
+        cost_estimate=pl.CostEstimate(flops=0, bytes_accessed=70 * sent, transcendentals=0),
         name="exchange_tiles_%d" % number,
     )(*operands)
-    return recv
-
-
-def combine_kernel(rows_at, local_ct, cap_cols, update, place_ref, cols_ref, *refs):
+
+
+def combine_kernel(row_count, rows_at, local_ct, cap_cols, update, place_ref, cols_ref, *refs):
     step = pl.program_id(0)
     tiles = refs[: 2 * rows_at]
     front_ref = refs[2 * rows_at]
-    out_ref = refs[-1]
+    out_ref = refs[-2] if update else refs[-1]
     for at in range(rows_at):
         span = pl.ds(at * TILE, TILE)
         for ct in range(local_ct):
@@ -226,11 +303,23 @@
                 total = total + jnp.where(there, tile.astype(jnp.float32), 0.0)
             out_ref[0, span, lanes] = total
     if update:
-        left_ref, right_ref = refs[2 * rows_at + 1 : 2 * rows_at + 3]
+        right_ref = refs[2 * rows_at + 1]
+        shares = refs[2 * rows_at + 2 : 3 * rows_at + 2]
+        factor_ref = refs[-1]
+        lefts = []
+        panel_of = lax.broadcasted_iota(jnp.int32, (TILE, KW), 1) // PANEL
+        for at in range(rows_at):
+            values = shares[at][0, 0]
+            factor_ref[0, pl.ds(at * TILE, TILE), :] = values
+            tile_no = lax.axis_index("row") + row_count * (step * rows_at + at)
+            lefts.append(
+                jnp.where(tile_no >= 2 * panel_of + 2, values, 0.0).astype(jnp.bfloat16)
+            )
+        left = jnp.concatenate(lefts, axis=0)
         for ct in range(0, local_ct, 2):
             lanes = pl.ds(ct * TILE, 2 * TILE)
             out_ref[0, :, lanes] -= lax.dot_general(
-                left_ref[...], right_ref[:, lanes], (((1,), (0,)), ((), ())),
+                left, right_ref[:, lanes], (((1,), (0,)), ((), ())),
                 preferred_element_type=jnp.float32,
             )
 
@@ -241,10 +330,6 @@
     cap_rows, cap_cols = recv.shape[2:4]
     width = front_block.shape[2]
     local_ct = width // TILE
-
-    def tile_map(at, sib, step, place_ref, cols_ref):
-        tile = step * rows_at + at
-        return (place_ref[0, sib, tile], place_ref[1, sib, tile], place_ref[2, sib, tile], 0, 0, 0)
 
     recv = recv.reshape(2, row_count * 2, quarter, cap_rows, cap_cols, TILE, TILE)
     recv = recv.reshape(4 * row_count, quarter, cap_rows, cap_cols, TILE, TILE)
@@ -264,19 +349,33 @@
     in_specs.append(pl.BlockSpec((1, rows_at * TILE, width), lambda step, *_: (0, step, 0)))
     operands = [recv] * (2 * rows_at) + [front_block]
     if factors is not None:
-        in_specs.append(pl.BlockSpec((rows_at * TILE, KW), lambda step, *_: (step, 0)))
+        right, shares = factors
+        ratio = col_count // row_count
+
+        def share_map(at, step, *_):
+            tile = step * rows_at + at
+            return (tile % ratio, tile // ratio, 0, 0)
+
         in_specs.append(pl.BlockSpec((KW, width), lambda step, *_: (0, 0)))
-        operands += list(factors)
+        for at in range(rows_at):
+            in_specs.append(pl.BlockSpec((1, 1, TILE, KW), functools.partial(share_map, at)))
+        operands += [right] + [shares] * rows_at
+    row_block = lambda step, *_: (0, step, 0)
+    out_shape = jax.ShapeDtypeStruct((1, row_tiles * TILE, width), jnp.float32)
+    out_specs = pl.BlockSpec((1, rows_at * TILE, width), row_block)
+    if factors is not None:
+        out_shape = (out_shape, jax.ShapeDtypeStruct((1, row_tiles * TILE, KW), jnp.float32))
+        out_specs = (out_specs, pl.BlockSpec((1, rows_at * TILE, KW), row_block))
     return pl.pallas_call(
-        functools.partial(combine_kernel, rows_at, local_ct, cap_cols, factors is not None),
+        functools.partial(combine_kernel, row_count, rows_at, local_ct, cap_cols, factors is not None),
         grid_spec=pltpu.PrefetchScalarGridSpec(
             num_scalar_prefetch=2,
             grid=(row_tiles // rows_at,),
             in_specs=in_specs,
-            out_specs=pl.BlockSpec((1, rows_at * TILE, width), lambda step, *_: (0, step, 0)),
+            out_specs=out_specs,
         ),
-        out_shape=jax.ShapeDtypeStruct((1, row_tiles * TILE, width), jnp.float32),
-        compiler_params=pltpu.CompilerParams(vmem_limit_bytes=48 * 2**20),
+        out_shape=out_shape,
+        compiler_params=pltpu.CompilerParams(vmem_limit_bytes=54 * 2**20),
         name="combine_update" if factors is not None else "combine_pivot_rows",
     )(place, cols, *operands)
 
@@ -365,55 +464,55 @@
     col_where = jnp.sum(jnp.where(col_hit, col_place + 1, 0), axis=-1).astype(jnp.int32) - 1
 
     early = min(pivot_tiles, cap_rows)
-    recv = exchange(outgoing, None, None, sizes, 0, early, 1)
+    bulk = cap_rows - early
+    cuts = [early + bulk * at // 3 for at in range(4)]
+    recv = exchange(outgoing, None, None, [], sizes, 0, early, 1)[0]
     pivot_rows = combine(
         recv, front_orig, place, col_where, sizes, pivot_tiles, 1, None
     )[0]
     gathered = lax.all_gather(pivot_rows.reshape(pivot_tiles, TILE, -1), "row", axis=0)
     gathered = gathered.swapaxes(0, 1).reshape(row_count * pivot_tiles * TILE, -1)[:KW]
-    corner = lax.all_gather(gathered[:, :TILE], "col", axis=0)[:KT]
-    diagonal = corner.swapaxes(0, 1).reshape(KW, KW)
-
-    if early < cap_rows:
-        middle = (cap_rows - early) // 2
-        recv = exchange(outgoing, recv, pivot_rows, sizes, early, middle, 2)
-
-    eye = jnp.eye(PANEL, dtype=jnp.float32)
-    dot = functools.partial(jnp.dot, precision=HI, preferred_element_type=jnp.float32)
-    low0 = jnp.linalg.cholesky(diagonal[:PANEL, :PANEL])
-    inv0 = jax.scipy.linalg.solve_triangular(low0, eye, lower=True)
-    g10 = dot(diagonal[PANEL:, :PANEL], inv0.T)
-    low1 = jnp.linalg.cholesky(diagonal[PANEL:, PANEL:] - dot(g10, g10.T))
-    inv1 = jax.scipy.linalg.solve_triangular(low1, eye, lower=True)
-
-    g0 = dot(inv0, gathered[:PANEL])
-    g1 = dot(inv1, gathered[PANEL:] - dot(g10, g0))
-    col_tiles = jnp.repeat(col_tile, TILE)
-    g1 = jnp.where((col_tiles >= 2)[None, :], g1, 0.0)
-    mine = jnp.concatenate([g0, g1], axis=0).T
-    trail0 = jnp.where((col_tiles >= 2)[None, :], g0, 0.0)
-    trail1 = jnp.where((col_tiles >= 4)[None, :], g1, 0.0)
-    right = jnp.concatenate([trail0, trail1], axis=0).astype(jnp.bfloat16)
+    corner = pivot_rows[:, :TILE].reshape(pivot_tiles, TILE, TILE)
+    corner = lax.all_gather(corner, ("row", "col"), axis=0)
+    corner = corner.reshape(row_count, col_count, pivot_tiles, TILE, TILE)[:, :KT]
+    diagonal = corner.transpose(2, 0, 3, 1, 4).reshape(-1, KW)[:KW]
+
+    if bulk >= 3:
+        recv = exchange(
+            outgoing, recv, None, [pivot_rows], sizes, cuts[0], cuts[1] - cuts[0], 2
+        )[0]
+        recv, _, inverse = exchange(
+            outgoing, recv, diagonal, [], sizes, cuts[1], cuts[2] - cuts[1], 3
+        )
+    else:
+        inverse = factor_alone(diagonal)
+
+    col_tiles = jnp.repeat(col_tile, TILE)[None, :]
+    mine = lax.dot_general(
+        inverse, gathered, (((1,), (0,)), ((), ())),
+        precision=HI, preferred_element_type=jnp.float32,
+    )
+    panel_of = jnp.arange(KW)[:, None] // PANEL
+    mine = jnp.where(col_tiles >= 2 * panel_of, mine, 0.0)
+    right = jnp.where(col_tiles >= 2 * panel_of + 2, mine, 0.0).astype(jnp.bfloat16)
 
     groups = [[q * row_count + h for h in range(row_count)] for q in range(ratio)]
-    share = mine.reshape(row_count, local_ct * TILE // row_count, KW)
+    share = mine.T.reshape(row_count, local_ct * TILE // row_count, KW)
     share = lax.all_to_all(
         share, "col", split_axis=0, concat_axis=0, axis_index_groups=groups, tiled=True
     )
     share = lax.dynamic_index_in_dim(share, row_id, 0, keepdims=False)
     whole = lax.all_gather(share, "col", axis=0)
-
-    if early < cap_rows:
-        recv = exchange(outgoing, recv, share, sizes, early + middle, cap_rows - early - middle, 3)
-
-    factor = (
-        whole.reshape(ratio, local_ct, TILE, KW).swapaxes(0, 1).reshape(local_rt * TILE, KW)
-    )
-    row_tiles = jnp.repeat(row_tile, TILE)[:, None]
-    panel_of = jnp.arange(KW)[None, :] // PANEL
-    left = jnp.where(row_tiles >= 2 * panel_of + 2, factor, 0.0).astype(jnp.bfloat16)
-    front = combine(recv, front_orig, place, col_where, sizes, local_rt, 2, (left, right))
-    return (front, factor[None])
+    if bulk >= 3:
+        recv = exchange(
+            outgoing, recv, None, [share], sizes, cuts[2], cuts[3] - cuts[2], 4
+        )[0]
+    elif bulk:
+        recv = exchange(outgoing, recv, None, [share], sizes, early, bulk, 5)[0]
+    return combine(
+        recv, front_orig, place, col_where, sizes, local_rt, 2,
+        (right, whole.reshape(ratio, local_ct, TILE, KW)),
+    )
 
 
 def solution(mesh):

time: 935 us -> 675 us (0.72); the launches traced: 922 us -> 673 us
  other arithmetic: 138 us -> 7.22 us
  waiting for transfers between devices: 70.3 us -> 0.75 us
  local copies, waits for them, and re-layouts: 54.2 us -> 10.5 us
  matrix products: 24 us -> 8.15 us
    another operation x19 -> x0, other arithmetic: 123 us -> none  [the longest x7 41.9 us: per_device(): low1 = jnp.linalg.cholesky(diagonal[PANEL:, PANEL:] - dot(g10, g10.T))]
    all_gather x1, waiting for transfers between devices: 44.5 us -> 0.02 us  [per_device(): lax.all_gather(pivot_rows.reshape(pivot_tiles, TILE, -1), 'row', axis=0)]
    all_gather x1, waiting for transfers between devices: 25.8 us -> 0.01 us  [per_device(): corner = lax.all_gather(corner, ('row', 'col'), axis=0)]
    another operation x19 -> x0, local copies, waits for them, and re-layouts: 20.2 us -> none  [the longest x9 8.98 us: per_device(): inv0 = jax.scipy.linalg.solve_triangular(low0, eye, lower=True)]
    another operation x10 -> x0, matrix products: 13.2 us -> none  [the longest x3 3.6 us: per_device(): inv1 = jax.scipy.linalg.solve_triangular(low1, eye, lower=True)]
    transpose x2, local copies, waits for them, and re-layouts: 14.6 us -> 1.97 us  [per_device(): diagonal = corner.transpose(2, 0, 3, 1, 4).reshape(-1, KW)[:KW]]
    pallas_call x6 -> x7, Pallas kernels: 610 us -> 616 us  [the longest x4 552 us: exchange(): pl.pallas_call(functools.partial(exchange_kernel, sizes, low, count, len(...]
  transfers between devices with their start and end apart: 3 -> 3, of which waited for: 2 -> 0; matrix products, arithmetic and copies ran while one was open for 0% -> 1% of each run, Pallas kernels for 47% -> 65%
where the time goes in v2:
time: 675 us; the launch traced here: 673 us
  Pallas kernels  616 us (91%)
  blocking collectives  15.9 us (2%)
  between operations  14 us (2%)
  local copies, waits for them, and re-layouts  10.5 us (2%)
  matrix products  8.15 us (1%)
  other arithmetic  7.22 us (1%)
    pallas_call x4, Pallas kernels, exchange(): pl.pallas_call(functools.partial(exchange_kernel, sizes, low, count, len(...  552 us
    pallas_call x2, Pallas kernels, combine(): pl.pallas_call(functools.partial(combine_kernel, row_count, rows_at, loca...  48.8 us
    all_to_all x1, blocking collectives, per_device(): lax.all_to_all(share, 'col', split_axis=0, concat_axis=0, axis_index_grou...  15.9 us
    pallas_call x1, Pallas kernels, pack(): pl.pallas_call(body, grid_spec=pltpu.PrefetchScalarGridSpec(num_scalar_pr...  15.6 us
  transfers between devices with their start and end apart: 3, of which 0 were waited for; matrix products, arithmetic and copies ran while one was open for 1% of the time, Pallas kernels for 65%

profile of v2, /device:TPU:25, one launch (start us, length us, event | category | flops | bytes accessed | tf_op | source)
XLA Modules:
  0.0 673.0 jit_solution(7062135641007083394)
XLA Ops:
  7.3 0.7 and_select_fusion
  8.0 0.8 fusion.13
  9.0 0.7 dynamic-slice_bitcast_fusion.1
  9.8 1.0 convert_reduce_fusion
  10.8 0.8 fusion.16
  12.8 15.6 %pack_tiles.1.refs_0_ = bf16[16,8,4,128,128]{4,3,2,1,0:T(8,128)(2,1)} custom-call(s32[2,8]{1,0:T(2,128)S(1)} %reshape.309.rows_ref, s32[32]{0:T(128)S(1)} %select_reduce_fusion.cols_ref, bf16[2048,4096]{1,0:T(8,128)(2,1)} %refs_1_.1, bf16[2048,4096]{1,0:T(8,128)(2,1)} %refs_1_.1), custom_call_target="tpu_custom_call" | custom-call | tf_op jit(solution)/shard_map/pack_tiles/pallas_call | solution.py:36
  28.3 115.3 %exchange_tiles_1.1 = (bf16[2,8,8,4,128,128]{5,4,3,2,1,0:T(8,128)(2,1)}, bf16[8,2,4,128,128]{4,3,2,1,0:T(8,128)(2,1)}) custom-call(bf16[16,8,4,128,128]{4,3,2,1,0:T(8,128)(2,1)} %pack_tiles.1.refs_0_), custom_call_target="tpu_custom_call" | custom-call | bytes 293601280 | tf_op jit(solution)/shard_map/exchange_tiles_1/pallas_call | solution.py:266
  143.9 0.7 pad_add_fusion.place_ref
  144.5 3.3 combine_pivot_rows.1
  147.9 1.6 slice.8
  149.5 0.7 all-gather.6.cloned.1.call-update
  150.2 126.2 %exchange_tiles_2.1 = (bf16[2,8,8,4,128,128]{5,4,3,2,1,0:T(8,128)(2,1)}, bf16[8,2,4,128,128]{4,3,2,1,0:T(8,128)(2,1)}) custom-call(bf16[16,8,4,128,128]{4,3,2,1,0:T(8,128)(2,1)} %pack_tiles.1.refs_0_, f32[256,1536]{1,0:T(8,128)} %bitcast.52, bf16[2,8,8,4,128,128]{5,4,3,2,1,0:T(8,128)(2,1)} %get-tuple-element.7.refs_2_), custom_call_target="tpu_custom_call", output_to_operand_aliasing={{0}: (2, {})} | custom-call | bytes 293601280 | tf_op jit(solution)/shard_map/exchange_tiles_2/pallas_call | solution.py:266
  276.5 1.3 slice_bitcast_fusion
  277.8 0.7 copy.16
  278.5 1.1 copy.22
  279.6 108.8 %exchange_tiles_3.1 = (bf16[2,8,8,4,128,128]{5,4,3,2,1,0:T(8,128)(2,1)}, bf16[8,2,4,128,128]{4,3,2,1,0:T(8,128)(2,1)}, f32[512,512]{1,0:T(8,128)}) custom-call(bf16[16,8,4,128,128]{4,3,2,1,0:T(8,128)(2,1)} %pack_tiles.1.refs_0_, f32[512,512]{1,0:T(8,128)} %bitcast.54, ...), custom_call_target="tpu_custom_call", output_to_operand_aliasing={{0}: (2, {})} | custom-call | bytes 293601280 | tf_op jit(solution)/shard_map/exchange_tiles_3/pallas_call | solution.py:266
  388.4 8.2 %bitcast_select_fusion = (f32[1536,512]{0,1:T(8,128)S(1)}, bf16[512,1536]{1,0:T(8,128)(2,1)}) fusion(s32[1536]{0:T(1024)S(1)} %broadcast_bitcast_fusion, s32[512]{0:T(512)S(1)} %fusion.4, f32[512,512]{1,0:T(8,128)} %get-tuple-element.9, f32[512,1536]{1,0:T(8,128)} %bitcast.56), kind=kOutput, calls=%fused_computation | convolution fusion | flops 4834197504 | bytes 8921088 | tf_op jit(solution)/shard_map/dot_general | solution.py:491
  396.5 2.4 copy.19
  398.9 15.9 %all_to_all.5 = f32[2,768,512]{2,1,0:T(8,128)S(1)} all-to-all(f32[2,768,512]{2,1,0:T(8,128)} %bitcast.53), channel_id=1, replica_groups={{0,1},{2,3},{4,5},{6,7},{8,9},{10,11},{12,13},{14,15},{16,17},{18,19},{..., dimensions={0} | all-to-all | bytes 6291456 | tf_op jit(solution)/shard_map/all_to_all | solution.py:501
  414.8 1.3 constant_dynamic-slice_fusion
  416.1 1.3 fusion.23.refs_1_
  417.4 201.8 %exchange_tiles_4.1 = (bf16[2,8,8,4,128,128]{5,4,3,2,1,0:T(8,128)(2,1)}, bf16[8,2,4,128,128]{4,3,2,1,0:T(8,128)(2,1)}) custom-call(bf16[16,8,4,128,128]{4,3,2,1,0:T(8,128)(2,1)} %pack_tiles.1.refs_0_, f32[768,512]{1,0:T(8,128)} %fusion.23.refs_1_, bf16[2,8,8,4,128,128]{5,4,3,2,1,0:T(8,128)(2,1)} %get-tuple-element.10.refs_2_), custom_call_target="tpu_custom_call", output_to_operand_aliasing={{0}: (2, {})} | custom-call | bytes 293601280 | tf_op jit(solution)/shard_map/exchange_tiles_4/pallas_call | solution.py:266
  619.2 1.8 select_convert_fusion.refs_5_
  621.0 45.5 %combine_update.1 = (f32[1,6144,1536]{2,1,0:T(8,128)}, f32[1,6144,512]{2,1,0:T(8,128)}) custom-call(s32[4,2,48]{2,1,0:T(2,128)} %pad_add_fusion.place_ref, s32[2,12]{1,0:T(2,128)} %broadcast_add_fusion.1.cols_ref, bf16[8,2,8,4,128,128]{5,4,3,2,1,0:T(8,128)(2,1)} %bitcast.44, bf16[8,2,8,4,128,128]{5,4,3,2,1,0:T(8,128)(2,1)} %bitcast.45, ...), custom_call_target="tpu_custom_call" | custom-call | tf_op jit(solution)/shard_map/combine_update/pallas_call | solution.py:369
  (28 shorter events, 2.0 us)
Async XLA Ops:
  7.2 269.3 %all-gather.4.cloned.1.call-start = ((), (), s32[]{:S(2)}) async-start(), calls=%async_computation.1 | async-start | bytes 2228224 | tf_op jit(solution)/shard_map/all_gather | solution.py:476
  149.4 238.9 %all-gather.6.cloned.1.call-start = ((), (), s32[]{:S(2)}) async-start(), calls=%async_computation.2 | async-start | bytes 4718592 | tf_op jit(solution)/shard_map/all_gather | solution.py:473
  150.2 470.8 %all-gather.8.cloned.1.call-start = ((), (), s32[]{:S(2)}) async-start(), calls=%async_computation.3 | async-start | bytes 14155776 | tf_op jit(solution)/shard_map/all_gather | solution.py:505
  417.4 201.8 %copy-start = (bf16[512,1536]{1,0:T(8,128)(2,1)S(1)}, bf16[512,1536]{1,0:T(8,128)(2,1)}, u32[]{:S(2)}) copy-start(bf16[512,1536]{1,0:T(8,128)(2,1)} %get-tuple-element.16) | copy-start | bytes 4718596
Sparse Core Ops, SparseCore 0:
  149.6 90.0 all-gather.3
  241.8 68.6 all-gather.5
  416.2 203.0 all-gather.7

commit v3 on v2

--- a/solution.py
+++ b/solution.py
@@ -465,7 +465,7 @@
 
     early = min(pivot_tiles, cap_rows)
     bulk = cap_rows - early
-    cuts = [early + bulk * at // 3 for at in range(4)]
+    cuts = [early, early + bulk // 3, cap_rows - max(1, bulk // 6), cap_rows]
     recv = exchange(outgoing, None, None, [], sizes, 0, early, 1)[0]
     pivot_rows = combine(
         recv, front_orig, place, col_where, sizes, pivot_tiles, 1, None
@@ -510,7 +510,7 @@
     elif bulk:
         recv = exchange(outgoing, recv, None, [share], sizes, early, bulk, 5)[0]
     return combine(
-        recv, front_orig, place, col_where, sizes, local_rt, 2,
+        recv, front_orig, place, col_where, sizes, local_rt, 4,
         (right, whole.reshape(ratio, local_ct, TILE, KW)),
     )
 

time: 675 us -> 674 us (level)
  waiting for transfers between devices: 0.75 us -> 50.7 us
  Pallas kernels: 616 us -> 569 us
    all_gather x1, waiting for transfers between devices: 0.01 us -> 50 us  [per_device(): whole = lax.all_gather(share, 'col', axis=0)]
    pallas_call x4, Pallas kernels: 552 us -> 510 us  [exchange(): pl.pallas_call(functools.partial(exchange_kernel, sizes, low, count, len(...]
  transfers between devices with their start and end apart: 3 -> 3, of which waited for: 0 -> 1; matrix products, arithmetic and copies ran while one was open for 1% -> 1% of each run, Pallas kernels for 65% -> 59%
where the time goes in v3:
time: 674 us; the launch traced here: 671 us
  Pallas kernels  569 us (84%)
  waiting for transfers between devices  50.7 us (8%)
  between operations  14 us (2%)
  blocking collectives  11.7 us (2%)
  local copies, waits for them, and re-layouts  10.5 us (2%)
  matrix products  8.18 us (1%)
  other arithmetic  7.28 us (1%)
    pallas_call x4, Pallas kernels, exchange(): pl.pallas_call(functools.partial(exchange_kernel, sizes, low, count, len(...  510 us
    all_gather x1, waiting for transfers between devices, per_device(): whole = lax.all_gather(share, 'col', axis=0)  50 us
    pallas_call x2, Pallas kernels, combine(): pl.pallas_call(functools.partial(combine_kernel, row_count, rows_at, loca...  43.1 us
    pallas_call x1, Pallas kernels, pack(): pl.pallas_call(body, grid_spec=pltpu.PrefetchScalarGridSpec(num_scalar_pr...  15.6 us
  transfers between devices with their start and end apart: 3, of which 1 were waited for; matrix products, arithmetic and copies ran while one was open for 1% of the time, Pallas kernels for 59%

profile of v3, /device:TPU:25, one launch (start us, length us, event | category | flops | bytes accessed | tf_op | source)
XLA Modules:
  0.0 671.5 jit_solution(13583574122452690136)
XLA Ops:
  7.3 0.7 and_select_fusion
  8.0 0.8 fusion.13
  9.0 0.7 dynamic-slice_bitcast_fusion.1
  9.8 1.0 convert_reduce_fusion
  10.8 0.8 fusion.16
  12.8 15.6 %pack_tiles.1.refs_0_ = bf16[16,8,4,128,128]{4,3,2,1,0:T(8,128)(2,1)} custom-call(s32[2,8]{1,0:T(2,128)S(1)} %reshape.309.rows_ref, s32[32]{0:T(128)S(1)} %select_reduce_fusion.cols_ref, bf16[2048,4096]{1,0:T(8,128)(2,1)} %refs_1_.1, bf16[2048,4096]{1,0:T(8,128)(2,1)} %refs_1_.1), custom_call_target="tpu_custom_call" | custom-call | tf_op jit(solution)/shard_map/pack_tiles/pallas_call | solution.py:36
  28.4 115.3 %exchange_tiles_1.1 = (bf16[2,8,8,4,128,128]{5,4,3,2,1,0:T(8,128)(2,1)}, bf16[8,2,4,128,128]{4,3,2,1,0:T(8,128)(2,1)}) custom-call(bf16[16,8,4,128,128]{4,3,2,1,0:T(8,128)(2,1)} %pack_tiles.1.refs_0_), custom_call_target="tpu_custom_call" | custom-call | bytes 293601280 | tf_op jit(solution)/shard_map/exchange_tiles_1/pallas_call | solution.py:266
  144.6 3.3 combine_pivot_rows.1
  147.9 1.6 slice.8
  149.6 0.7 all-gather.6.cloned.1.call-update
  150.3 126.2 %exchange_tiles_2.1 = (bf16[2,8,8,4,128,128]{5,4,3,2,1,0:T(8,128)(2,1)}, bf16[8,2,4,128,128]{4,3,2,1,0:T(8,128)(2,1)}) custom-call(bf16[16,8,4,128,128]{4,3,2,1,0:T(8,128)(2,1)} %pack_tiles.1.refs_0_, f32[256,1536]{1,0:T(8,128)} %bitcast.58, bf16[2,8,8,4,128,128]{5,4,3,2,1,0:T(8,128)(2,1)} %get-tuple-element.7.refs_2_), custom_call_target="tpu_custom_call", output_to_operand_aliasing={{0}: (2, {})} | custom-call | bytes 293601280 | tf_op jit(solution)/shard_map/exchange_tiles_2/pallas_call | solution.py:266
  276.6 1.3 slice_bitcast_fusion
  277.9 0.7 copy.16
  278.6 1.0 copy.22
  279.6 167.7 %exchange_tiles_3.1 = (bf16[2,8,8,4,128,128]{5,4,3,2,1,0:T(8,128)(2,1)}, bf16[8,3,4,128,128]{4,3,2,1,0:T(8,128)(2,1)}, f32[512,512]{1,0:T(8,128)}) custom-call(bf16[16,8,4,128,128]{4,3,2,1,0:T(8,128)(2,1)} %pack_tiles.1.refs_0_, f32[512,512]{1,0:T(8,128)} %bitcast.60, ...), custom_call_target="tpu_custom_call", output_to_operand_aliasing={{0}: (2, {})} | custom-call | bytes 440401920 | tf_op jit(solution)/shard_map/exchange_tiles_3/pallas_call | solution.py:266
  447.4 8.2 %bitcast_select_fusion = (f32[1536,512]{0,1:T(8,128)S(1)}, bf16[512,1536]{1,0:T(8,128)(2,1)}) fusion(s32[1536]{0:T(1024)S(1)} %broadcast_bitcast_fusion, s32[512]{0:T(512)S(1)} %fusion.4, f32[512,512]{1,0:T(8,128)} %get-tuple-element.9, f32[512,1536]{1,0:T(8,128)} %bitcast.62), kind=kOutput, calls=%fused_computation | convolution fusion | flops 4834197504 | bytes 8921088 | tf_op jit(solution)/shard_map/dot_general | solution.py:491
  455.6 2.4 copy.19
  457.9 11.7 %all_to_all.5 = f32[2,768,512]{2,1,0:T(8,128)S(1)} all-to-all(f32[2,768,512]{2,1,0:T(8,128)} %bitcast.59), channel_id=1, replica_groups={{0,1},{2,3},{4,5},{6,7},{8,9},{10,11},{12,13},{14,15},{16,17},{18,19},{..., dimensions={0} | all-to-all | bytes 6291456 | tf_op jit(solution)/shard_map/all_to_all | solution.py:501
  469.7 1.3 constant_dynamic-slice_fusion
  470.9 1.3 fusion.23.refs_1_
  472.2 101.1 %exchange_tiles_4.1 = (bf16[2,8,8,4,128,128]{5,4,3,2,1,0:T(8,128)(2,1)}, bf16[8,1,4,128,128]{4,3,2,1,0:T(8,128)(2,1)}) custom-call(bf16[16,8,4,128,128]{4,3,2,1,0:T(8,128)(2,1)} %pack_tiles.1.refs_0_, f32[768,512]{1,0:T(8,128)} %fusion.23.refs_1_, bf16[2,8,8,4,128,128]{5,4,3,2,1,0:T(8,128)(2,1)} %get-tuple-element.10.refs_2_), custom_call_target="tpu_custom_call", output_to_operand_aliasing={{0}: (2, {})} | custom-call | bytes 146800640 | tf_op jit(solution)/shard_map/exchange_tiles_4/pallas_call | solution.py:266
  573.4 1.8 select_convert_fusion.refs_9_
  575.2 50.0 %all-gather.8.cloned.1.call-done = f32[8,768,512]{2,1,0:T(8,128)} async-done(((f32[1,768,512]{2,1,0:T(8,128)}), f32[8,768,512]{2,1,0:T(8,128)}) %all-gather.8.cloned.1.call-update) | async-done | bytes 12582928 | tf_op jit(solution)/shard_map/all_gather | solution.py:505
  625.2 39.8 %combine_update.1 = (f32[1,6144,1536]{2,1,0:T(8,128)}, f32[1,6144,512]{2,1,0:T(8,128)}) custom-call(s32[4,2,48]{2,1,0:T(2,128)} %pad_add_fusion.place_ref, s32[2,12]{1,0:T(2,128)} %broadcast_add_fusion.1.cols_ref, bf16[8,2,8,4,128,128]{5,4,3,2,1,0:T(8,128)(2,1)} %bitcast.44, bf16[8,2,8,4,128,128]{5,4,3,2,1,0:T(8,128)(2,1)} %bitcast.45, ...), custom_call_target="tpu_custom_call" | custom-call | tf_op jit(solution)/shard_map/combine_update/pallas_call | solution.py:369
  (28 shorter events, 2.7 us)
Async XLA Ops:
  7.2 269.4 %all-gather.4.cloned.1.call-start = ((), (), s32[]{:S(2)}) async-start(), calls=%async_computation.1 | async-start | bytes 2228224 | tf_op jit(solution)/shard_map/all_gather | solution.py:476
  149.5 297.9 %all-gather.6.cloned.1.call-start = ((), (), s32[]{:S(2)}) async-start(), calls=%async_computation.2 | async-start | bytes 4718592 | tf_op jit(solution)/shard_map/all_gather | solution.py:473
  150.3 474.9 %all-gather.8.cloned.1.call-start = ((), (), s32[]{:S(2)}) async-start(), calls=%async_computation.3 | async-start | bytes 14155776 | tf_op jit(solution)/shard_map/all_gather | solution.py:505
  472.2 101.1 %copy-start = (bf16[512,1536]{1,0:T(8,128)(2,1)S(1)}, bf16[512,1536]{1,0:T(8,128)(2,1)}, u32[]{:S(2)}) copy-start(bf16[512,1536]{1,0:T(8,128)(2,1)} %get-tuple-element.16) | copy-start | bytes 4718596
Sparse Core Ops, SparseCore 0:
  149.6 90.0 all-gather.3
  241.8 57.4 all-gather.5
  471.1 154.0 all-gather.7
